TPU v7x, 1024 devices: a whole 8x8x8 slice. The times are simulated.
1024 devices in a mesh: col: 64 (over z, x), row: 16 (over y, core).
Axes of the slice: x: 8, y: 8, z: 8, core: 2. Of those that a mesh axis runs over, the one named last changes fastest.
Arguments:
- weight: float32 [8192, 16384], P('row', 'col'), may hold values from -6 to 6
- momentum: float32 [8192, 16384], P('row', 'col'), may hold values from -6 to 6
- gradient: bfloat16 [8192, 16384], P('row', 'col'), may hold values from -6 to 6
- right_factor: float32 [16384, 256], P('col'), may hold values from -6 to 6
Outputs:
- new_weight: float32 [8192, 16384], P('row', 'col')
- new_momentum: float32 [8192, 16384], P('row', 'col')
- new_factor: float32 [16384, 256], P('col')
All inputs are finite; a program needn't handle non-finite values.
Results may differ from a plain program's by a relative error of at most 0.0003.
Values sent between devices are 32-bit elements; how exact they have to be, the bound alone decides.
A program may use at most 32 MiB of HBM per device.

v0:
```python
import jax
import jax.numpy as jnp
from jax import lax
from jax.sharding import PartitionSpec as P

D_IN = 16384


def contract(first, second, first_dim, second_dim):
    return lax.dot_general(
        first,
        second,
        (((first_dim,), (second_dim,)), ((), ())),
        precision=lax.Precision.HIGHEST,
        preferred_element_type=jnp.float32,
    )


def orthonormal(left_raw, gram_matrix):
    lower = jnp.linalg.cholesky(gram_matrix)
    return lax.linalg.triangular_solve(
        lower, left_raw, left_side=False, lower=True, transpose_a=True
    )


def on_device(weight, momentum, gradient, right_factor):
    combined = momentum + gradient.astype(jnp.float32)
    partial_value = contract(combined, right_factor, 1, 0)
    left_raw = lax.psum(partial_value, "col")
    gram_matrix = lax.psum(contract(left_raw, left_raw, 0, 0), "row")
    left_factor = orthonormal(left_raw, gram_matrix)
    right_raw = lax.psum(contract(combined, left_factor, 0, 0), "row")
    squares = lax.psum(jnp.sum(right_raw * right_raw, axis=0), "col")
    new_factor = right_raw / jnp.sqrt(squares / D_IN + 1e-06)
    new_momentum = combined - 0.05 * contract(left_factor, right_raw, 1, 1)
    new_weight = weight - 0.5 * contract(left_factor, new_factor, 1, 1)
    return (new_weight, new_momentum, new_factor)


def solution(mesh):
    in_specs = (P("row", "col"), P("row", "col"), P("row", "col"), P("col", None))
    out_specs = (P("row", "col"), P("row", "col"), P("col", None))
    return jax.shard_map(
        on_device, mesh=mesh, in_specs=in_specs, out_specs=out_specs, check_vma=False
    )
```

profile of v0, /device:TPU:48, one launch (start us, length us, event | category | flops | bytes accessed | tf_op | source)
XLA Modules:
  0.0 652.9 jit_solution(737107473114813237)
XLA Ops:
  7.2 0.0 copy-start
  7.2 0.0 all-reduce.5.cloned.1.call-start
  7.2 0.9 copy-done
  8.1 2.5 fusion.6
  10.6 0.0 all-reduce.5.cloned.1.call-update
  10.6 0.0 all-reduce.7.cloned.1.call-start
  10.7 181.6 %all-reduce.5.cloned.1.call-done = f32[512,256]{1,0:T(8,128)} async-done(((f32[512,256]{1,0:T(8,128)}), f32[512,256]{1,0:T(8,128)}) %all-reduce.5.cloned.1.call-update) | async-done | bytes 524304 | tf_op jit(solution)/shard_map/psum | solution.py:29
  192.3 2.9 fusion.16
  195.2 0.0 all-reduce.7.cloned.1.call-update
  195.2 0.0 all-reduce.9.cloned.1.call-start
  195.3 115.1 %all-reduce.7.cloned.1.call-done = f32[256,256]{0,1:T(8,128)} async-done(((f32[256,256]{0,1:T(8,128)}), f32[256,256]{0,1:T(8,128)}) %all-reduce.7.cloned.1.call-update) | async-done | bytes 262160 | tf_op jit(solution)/shard_map/psum | solution.py:30
  310.4 0.0 copy-start.5
  310.4 1.1 copy.8
  311.5 0.0 copy-done.5
  311.6 11.7 %cholesky.50 = f32[128,128]{1,0:T(8,128)S(1)} custom-call(f32[128,128]{1,0:T(8,128)S(1)} %cholesky.118), custom_call_target="Cholesky" | custom-call | tf_op jit(solution)/shard_map/jit(cholesky)/cholesky | solution.py:20
  323.4 9.8 %custom-call.14 = f32[1,128,128]{1,2,0:T(8,128)S(1)} custom-call(f32[1,128,128]{2,1,0:T(8,128)S(1)} %get-tuple-element.24), custom_call_target="InvertDiagBlocksLowerTriangular" | custom-call | tf_op jit(solution)/shard_map/jit(cholesky)/cholesky | solution.py:20
  333.2 0.2 constant_dynamic-update-slice_fusion.1
  333.4 0.3 convolution_subtract_fusion.1
  333.7 11.7 %cholesky.105 = f32[128,128]{1,0:T(8,128)S(1)} custom-call(f32[128,128]{1,0:T(8,128)S(1)} %convolution_subtract_fusion.1), custom_call_target="Cholesky" | custom-call | tf_op jit(solution)/shard_map/jit(cholesky)/cholesky | solution.py:20
  345.4 0.6 compare_reduce_fusion
  347.4 0.0 copy-start.2
  347.4 0.1 triangular_solve.58
  347.5 4.1 while.1
  347.6 0.6 fusion.27
  348.2 1.4 bitcast_dynamic-update-slice_fusion.2
  349.6 0.6 fusion.27
  350.2 1.4 bitcast_dynamic-update-slice_fusion.2
  351.6 19.7 %custom-call.15 = f32[2,128,128]{1,2,0:T(8,128)S(1)} custom-call(f32[2,128,128]{2,1,0:T(8,128)S(1)} %get-tuple-element.10), custom_call_target="InvertDiagBlocksLowerTriangular" | custom-call | tf_op jit(solution)/shard_map/triangular_solve | solution.py:21
  371.3 0.0 copy-done.2
  371.3 0.4 fusion.3
  371.7 0.0 copy-start.1
  371.8 0.6 convolution_subtract_fusion
  372.4 0.0 copy-start.4
  372.4 0.4 fusion.7
  372.8 0.0 copy-done.1
  372.8 0.5 copy-done.4
  373.4 1.7 fusion.2
  375.1 0.0 all-reduce.9.cloned.1.call-update
  375.1 121.2 %all-reduce.9.cloned.1.call-done = f32[256,256]{1,0:T(8,128)} async-done(((f32[256,256]{1,0:T(8,128)}), f32[256,256]{1,0:T(8,128)}) %all-reduce.9.cloned.1.call-update) | async-done | bytes 262160 | tf_op jit(solution)/shard_map/psum | solution.py:32
  496.3 0.0 copy-start.3
  496.3 1.1 multiply_reduce_fusion
  497.4 145.3 %psum.31 = f32[256]{0:T(256)S(1)} all-reduce(f32[256]{0:T(256)S(1)} %multiply_reduce_fusion), channel_id=1, replica_groups=mesh['col'=64,'row'=16] {'col'}, use_global_device_ids=true, to_apply=%region_8.9 | all-reduce | flops 256 | bytes 2048 | tf_op jit(solution)/shard_map/psum | solution.py:33
  642.7 0.0 copy-done.3
  642.8 0.0 copy-done.7
  642.8 0.0 copy-start.6
  642.8 1.8 fusion.1
  644.6 0.0 copy-done.6
  644.6 1.8 fusion
  (13 shorter events, 0.2 us)
Async XLA Ops:
  7.2 1.0 copy-start
  7.2 185.1 %all-reduce.5.cloned.1.call-start = ((), (), s32[]{:S(2)}) async-start(), calls=%async_computation | async-start | bytes 1048576 | tf_op jit(solution)/shard_map/psum | solution.py:29
  10.6 299.7 %all-reduce.7.cloned.1.call-start = ((), (), s32[]{:S(2)}) async-start(), calls=%async_computation.1 | async-start | bytes 524288 | tf_op jit(solution)/shard_map/psum | solution.py:30
  195.2 301.1 %all-reduce.9.cloned.1.call-start = ((), (), s32[]{:S(2)}) async-start(), calls=%async_computation.2 | async-start | bytes 524288 | tf_op jit(solution)/shard_map/psum | solution.py:32
  310.4 1.2 copy-start.5
  347.4 23.9 %copy-start.2 = (f32[512,256]{1,0:T(8,128)S(1)}, f32[512,256]{1,0:T(8,128)}, u32[]{:S(2)}) copy-start(f32[512,256]{1,0:T(8,128)} %all-reduce.5.cloned.1.call-done) | copy-start | bytes 1572868
  371.7 1.0 copy-start.1
  372.4 1.0 copy-start.4
  496.3 146.4 %copy-start.3 = (f32[256,256]{1,0:T(8,128)S(1)}, f32[256,256]{1,0:T(8,128)}, u32[]{:S(2)}) copy-start(f32[256,256]{1,0:T(8,128)} %all-reduce.9.cloned.1.call-done) | copy-start | bytes 786436
  496.3 146.5 %copy-start.7 = (f32[512,256]{1,0:T(8,128)S(1)}, f32[512,256]{1,0:T(8,128)}, u32[]{:S(2)}) copy-start(f32[512,256]{1,0:T(8,128)} %param.4) | copy-start | bytes 1572868
  642.8 1.8 copy-start.6
Sparse Core Ops, SparseCore 0:
  11.8 180.4 all-reduce.4
  195.3 115.0 all-reduce.6
  375.2 121.0 all-reduce.8
where the time goes:
time: 653 us
  waiting for transfers between devices  418 us (64%)
  blocking collectives  145 us (22%)
  other arithmetic  54.8 us (8%)
  between operations  15.2 us (2%)
  matrix products  12.6 us (2%)
  local copies, waits for them, and re-layouts  6.67 us (1%)
    psum x1, waiting for transfers between devices, on_device(): left_raw = lax.psum(partial_value, 'col')  182 us
    psum x1, blocking collectives, on_device(): squares = lax.psum(jnp.sum(right_raw * right_raw, axis=0), 'col')  145 us
    psum x1, waiting for transfers between devices, on_device(): right_raw = lax.psum(contract(combined, left_factor, 0, 0), 'row')  121 us
    psum x1, waiting for transfers between devices, on_device(): gram_matrix = lax.psum(contract(left_raw, left_raw, 0, 0), 'row')  115 us
    another operation x6, other arithmetic, orthonormal(): lower = jnp.linalg.cholesky(gram_matrix)  34 us
    another operation x3, other arithmetic, orthonormal(): lax.linalg.triangular_solve(lower, left_raw, left_side=False, lower=True,...  19.7 us
  transfers between devices with their start and end apart: 3, of which 3 were waited for; matrix products, arithmetic and copies ran while one was open for 0% of the time, Pallas kernels for 0%

commit v1 on v0

v1 whole, which is shorter than its diff:
```python
import functools
import math

import jax
import jax.numpy as jnp
from jax import lax
from jax.experimental import pallas as pl
from jax.experimental.pallas import tpu as pltpu
from jax.sharding import PartitionSpec as P

D_IN = 16384
RANK = 256
LANES = 128
MESH = pl.DeviceIdType.MESH
F32 = jnp.float32

OUT_X, OUT_Z, IN_X, IN_Z, BACK_Z, BACK_X, ALL_X, ALL_Z, GRAM, GRAM_ALL, RIGHT, RIGHT_ALL, SQUARES = range(13)


def dot(first, second, first_dim, second_dim):
    return lax.dot_general(
        first,
        second,
        (((first_dim,), (second_dim,)), ((), ())),
        precision=lax.Precision.HIGHEST,
        preferred_element_type=F32,
    )


def iota(shape, dim):
    return lax.broadcasted_iota(jnp.int32, shape, dim)


def inverse_factor(work, block, inner):
    n = work.shape[0]

    def step(index, carry):
        panel = work[0:block, :]
        lane = iota((block, n), 1)
        sub = iota((block, n), 0)
        narrow = iota((block, LANES), 0)
        row_lane = iota((1, n), 1)
        for start in range(0, block, inner):
            columns = [
                jnp.broadcast_to(panel[:, start + j : start + j + 1], (block, LANES)) for j in range(inner)
            ]
            for j in range(inner):
                k = start + j
                scale = lax.rsqrt(columns[j][k : k + 1, :])
                factor = jnp.where(narrow > k, columns[j] * scale, 0.0)
                row = jnp.where(row_lane == k, 1.0, panel[k : k + 1, :])
                row = row * jnp.concatenate([scale] * (n // LANES), axis=1)
                for later in range(j + 1, inner):
                    columns[later] = columns[later] - factor * (columns[later][k : k + 1, :] * scale)
                wide = jnp.concatenate([factor] * (n // LANES), axis=1)
                below = jnp.where((lane == k) & (sub > k), 0.0, panel) - wide * row
                panel = jnp.where(sub == k, jnp.broadcast_to(row, (block, n)), below)
        left = n - block * index
        own = jnp.where((lane > sub) & (lane < left), 0.0, panel)
        right_side = jnp.where((lane < block) & (lane > sub), 0.0, panel)
        left_side = jnp.where((lane < left) & (lane >= block), panel, 0.0)
        update = dot(left_side[:, block:], right_side, 0, 0)
        rest_lane = iota((n - block, n), 1)
        rest_sub = iota((n - block, n), 0) + block
        rest = jnp.where((rest_lane < block) & (rest_sub < left), 0.0, work[block:, :]) - update
        work[0 : n - block, :] = pltpu.roll(rest, n - block, 1)
        work[n - block :, :] = pltpu.roll(own, n - block, 1)
        return carry

    lax.fori_loop(0, n // block, step, 0)


def kernel(
    side, depth, weight_hbm, momentum_hbm, gradient_hbm, factor_hbm, new_weight_hbm, new_momentum_hbm, new_factor_hbm,
    weight, momentum, gradient, factor, combined, partial, scatter_in, middle, middle_in, left, gram, gram_in, gram_all,
    work, right, right_in, right_all, squares, squares_in, new_weight, new_momentum, new_factor,
    load_sem, store_sem, send_sem, recv_sem,
):
    rows = partial.shape[1]
    big, small = rows // side, rows // side // side
    col, row = lax.axis_index("col"), lax.axis_index("row")
    z, x = lax.div(col, side), lax.rem(col, side)
    far = sorted(range(1, side), key=lambda k: -min(k, side - k))
    far_row = sorted(range(1, 2 * depth), key=lambda k: -min(k // 2, depth - k // 2))

    def x_peer(k):
        return lax.rem(x + k, side)

    def z_peer(k):
        return lax.rem(z + k, side)

    def at(z_of, x_of):
        return (z_of * side + x_of, row)

    def row_peer(k):
        return lax.rem(row + k, 2 * depth)

    def send(source, target, batch, device):
        pltpu.make_async_remote_copy(
            src_ref=source,
            dst_ref=target,
            send_sem=send_sem.at[batch],
            recv_sem=recv_sem.at[batch],
            device_id=device,
            device_id_type=MESH,
        ).start()

    def arrived(target, batch):
        pltpu.make_async_copy(target, target, recv_sem.at[batch]).wait()

    def sent(source, batch):
        pltpu.make_async_copy(source, source, send_sem.at[batch]).wait()

    barrier = pltpu.get_barrier_semaphore()
    for k in far:
        pl.semaphore_signal(barrier, inc=1, device_id=at(z, x_peer(k)), device_id_type=MESH)
        pl.semaphore_signal(barrier, inc=1, device_id=at(z_peer(k), x), device_id_type=MESH)
    for k in far_row:
        pl.semaphore_signal(barrier, inc=1, device_id=(col, row_peer(k)), device_id_type=MESH)

    loads = [
        pltpu.make_async_copy(source, target, load_sem.at[i])
        for i, (source, target) in enumerate(
            ((momentum_hbm, momentum), (gradient_hbm, gradient), (factor_hbm, factor), (weight_hbm, weight))
        )
    ]
    for load in loads:
        load.start()
    for load in loads[:3]:
        load.wait()
    combined[...] = momentum[...] + gradient[...].astype(F32)
    product = dot(combined[...], factor[...], 1, 0)
    partial[0] = product[:, :LANES]
    partial[1] = product[:, LANES:]

    pl.semaphore_wait(barrier, 2 * len(far) + len(far_row))

    for k in far:
        send(partial.at[0, pl.ds(x_peer(k) * big, big)], scatter_in.at[0, k], OUT_X, at(z, x_peer(k)))
        send(partial.at[1, pl.ds(z_peer(k) * big, big)], scatter_in.at[1, k], OUT_Z, at(z_peer(k), x))
    arrived(scatter_in.at[0, pl.ds(1, side - 1)], OUT_X)
    middle[0] = partial[0, pl.ds(x * big, big)] + jnp.sum(scatter_in[0, 1:], axis=0)
    for k in far:
        send(middle.at[0, pl.ds(z_peer(k) * small, small)], middle_in.at[0, k], IN_Z, at(z_peer(k), x))
    arrived(scatter_in.at[1, pl.ds(1, side - 1)], OUT_Z)
    middle[1] = partial[1, pl.ds(z * big, big)] + jnp.sum(scatter_in[1, 1:], axis=0)
    for k in far:
        send(middle.at[1, pl.ds(x_peer(k) * small, small)], middle_in.at[1, k], IN_X, at(z, x_peer(k)))

    first = pl.ds(x * big + z * small, small)
    second = pl.ds(z * big + x * small, small)
    arrived(middle_in.at[0, pl.ds(1, side - 1)], IN_Z)
    left[0, first] = middle[0, pl.ds(z * small, small)] + jnp.sum(middle_in[0, 1:], axis=0)
    for k in far:
        send(left.at[0, first], left.at[0, first], BACK_Z, at(z_peer(k), x))
    arrived(middle_in.at[1, pl.ds(1, side - 1)], IN_X)
    left[1, second] = middle[1, pl.ds(x * small, small)] + jnp.sum(middle_in[1, 1:], axis=0)
    for k in far:
        send(left.at[1, second], left.at[1, second], BACK_X, at(z, x_peer(k)))
    arrived(left.at[0, pl.ds(0, big - small)], BACK_Z)
    for k in far:
        block = pl.ds(x * big, big)
        send(left.at[0, block], left.at[0, block], ALL_X, at(z, x_peer(k)))
    arrived(left.at[1, pl.ds(0, big - small)], BACK_X)
    for k in far:
        block = pl.ds(z * big, big)
        send(left.at[1, block], left.at[1, block], ALL_Z, at(z_peer(k), x))
    arrived(left.at[0, pl.ds(0, rows - big)], ALL_X)
    arrived(left.at[1, pl.ds(0, rows - big)], ALL_Z)

    left_raw = jnp.concatenate([left[0], left[1]], axis=1)
    gram[0:RANK] = dot(left_raw, left[0], 0, 0)
    gram[RANK:] = dot(left_raw, left[1], 0, 0)
    tile_rows = 2 * RANK // (side * side)
    tile = pl.ds(col * tile_rows, tile_rows)
    gram_in[row] = gram[tile]
    for k in far_row:
        send(gram.at[tile], gram_in.at[row], GRAM, (col, row_peer(k)))

    right[...] = dot(combined[...], left_raw, 0, 0)
    strip_rows = RANK // (2 * depth)
    strip = pl.ds(row * strip_rows, strip_rows)
    for k in far_row:
        send(right.at[pl.ds(row_peer(k) * strip_rows, strip_rows)], right_in.at[k], RIGHT, (col, row_peer(k)))

    arrived(gram_in.at[pl.ds(0, 2 * depth - 1)], GRAM)
    gram_all[tile] = jnp.sum(gram_in[...], axis=0)

    def plane(start):
        def one(j, carry):
            dz, dx = far_of(lax.div(j, side)), far_of(lax.rem(j, side))
            start(at(lax.rem(z + dz, side), lax.rem(x + dx, side)))
            return carry

        lax.fori_loop(0, side * side - 1, one, 0)

    def far_of(j):
        half = lax.div(j + 1, 2)
        return side // 2 + jnp.where(lax.rem(j, 2) == 1, -half, half)

    plane(lambda device: send(gram_all.at[tile], gram_all.at[tile], GRAM_ALL, device))

    arrived(right_in.at[pl.ds(1, 2 * depth - 1)], RIGHT)
    right_all[strip] = right[strip] + jnp.sum(right_in[1:], axis=0)
    for k in far_row:
        send(right_all.at[strip], right_all.at[strip], RIGHT_ALL, (col, row_peer(k)))

    arrived(gram_all.at[pl.ds(0, 2 * RANK - tile_rows)], GRAM_ALL)
    work[:, :LANES] = gram_all[0:RANK]
    work[:, LANES:] = gram_all[RANK:]
    inverse_factor(work, 64, 16)
    inverse = work[...]

    arrived(right_all.at[pl.ds(0, RANK - strip_rows)], RIGHT_ALL)
    right_raw = dot(right_all[...], inverse, 1, 1)
    sums = jnp.sum(right_raw * right_raw, axis=0, keepdims=True)
    squares[...] = jnp.zeros_like(squares)
    squares[0:1] = sums[:, :LANES]
    squares[1:2] = sums[:, LANES:]
    squares_in[col] = squares[...]
    plane(lambda device: send(squares, squares_in.at[col], SQUARES, device))

    left_factor = dot(left_raw, inverse, 1, 1)
    new_momentum[...] = combined[...] - 0.05 * dot(left_factor, right_raw, 1, 1)
    store_momentum = pltpu.make_async_copy(new_momentum, new_momentum_hbm, store_sem.at[0])
    store_momentum.start()
    loads[3].wait()

    arrived(squares_in.at[pl.ds(0, side * side - 1)], SQUARES)
    total = jnp.sum(squares_in[...], axis=0)
    total = jnp.concatenate([total[0:1], total[1:2]], axis=1)
    new_factor[...] = right_raw / jnp.sqrt(total / D_IN + 1e-06)
    store_factor = pltpu.make_async_copy(new_factor, new_factor_hbm, store_sem.at[1])
    store_factor.start()
    new_weight[...] = weight[...] - 0.5 * dot(left_factor, new_factor[...], 1, 1)
    store_weight = pltpu.make_async_copy(new_weight, new_weight_hbm, store_sem.at[2])
    store_weight.start()

    sent(scatter_in.at[0, pl.ds(1, side - 1)], OUT_X)
    sent(scatter_in.at[1, pl.ds(1, side - 1)], OUT_Z)
    sent(middle_in.at[0, pl.ds(1, side - 1)], IN_Z)
    sent(middle_in.at[1, pl.ds(1, side - 1)], IN_X)
    sent(left.at[0, pl.ds(0, big - small)], BACK_Z)
    sent(left.at[1, pl.ds(0, big - small)], BACK_X)
    sent(left.at[0, pl.ds(0, rows - big)], ALL_X)
    sent(left.at[1, pl.ds(0, rows - big)], ALL_Z)
    sent(gram_in.at[pl.ds(0, 2 * depth - 1)], GRAM)
    sent(gram_all.at[pl.ds(0, 2 * RANK - tile_rows)], GRAM_ALL)
    sent(right_in.at[pl.ds(1, 2 * depth - 1)], RIGHT)
    sent(right_all.at[pl.ds(0, RANK - strip_rows)], RIGHT_ALL)
    sent(squares_in.at[pl.ds(0, side * side - 1)], SQUARES)
    store_momentum.wait()
    store_factor.wait()
    store_weight.wait()


def on_device(side, depth, weight, momentum, gradient, right_factor):
    rows, columns = weight.shape
    big, small = rows // side, rows // side // side
    vmem = pltpu.VMEM
    scratch = [
        vmem((rows, columns), F32),
        vmem((rows, columns), F32),
        vmem((rows, columns), gradient.dtype),
        vmem((columns, RANK), F32),
        vmem((rows, columns), F32),
        vmem((2, rows, LANES), F32),
        vmem((2, side, big, LANES), F32),
        vmem((2, big, LANES), F32),
        vmem((2, side, small, LANES), F32),
        vmem((2, rows, LANES), F32),
        vmem((2 * RANK, LANES), F32),
        vmem((2 * depth, 2 * RANK // (side * side), LANES), F32),
        vmem((2 * RANK, LANES), F32),
        vmem((RANK, RANK), F32),
        vmem((columns, RANK), F32),
        vmem((2 * depth, columns // (2 * depth), RANK), F32),
        vmem((columns, RANK), F32),
        vmem((8, LANES), F32),
        vmem((side * side, 8, LANES), F32),
        vmem((rows, columns), F32),
        vmem((rows, columns), F32),
        vmem((columns, RANK), F32),
        pltpu.SemaphoreType.DMA((4,)),
        pltpu.SemaphoreType.DMA((3,)),
        pltpu.SemaphoreType.DMA((13,)),
        pltpu.SemaphoreType.DMA((13,)),
    ]
    return pl.pallas_call(
        functools.partial(kernel, side, depth),
        out_shape=(
            jax.ShapeDtypeStruct((rows, columns), F32),
            jax.ShapeDtypeStruct((rows, columns), F32),
            jax.ShapeDtypeStruct((columns, RANK), F32),
        ),
        in_specs=[pl.BlockSpec(memory_space=pl.ANY)] * 4,
        out_specs=(pl.BlockSpec(memory_space=pl.ANY),) * 3,
        scratch_shapes=scratch,
        compiler_params=pltpu.CompilerParams(
            collective_id=0, has_side_effects=True, vmem_limit_bytes=48 * 1024 * 1024
        ),
        name="dion_step",
    )(weight, momentum, gradient, right_factor)


def solution(mesh):
    side = math.isqrt(mesh.shape["col"])
    depth = mesh.shape["row"] // 2
    in_specs = (P("row", "col"), P("row", "col"), P("row", "col"), P("col", None))
    out_specs = (P("row", "col"), P("row", "col"), P("col", None))
    return jax.shard_map(
        functools.partial(on_device, side, depth), mesh=mesh, in_specs=in_specs, out_specs=out_specs, check_vma=False
    )
```

time: 653 us -> 87.9 us (0.13)
  the two profiles are of different devices: /device:TPU:48 before, /device:TPU:2 now
where the time goes in v1:
time: 87.9 us; the launch traced here: 87.6 us
  Pallas kernels  80.7 us (92%)
  local copies, waits for them, and re-layouts  6.27 us (7%)
    pallas_call x1, Pallas kernels, on_device(): pl.pallas_call(functools.partial(kernel, side, depth), out_shape=(jax.Sha...  80.7 us
    unnamed x11, local copies, waits for them, and re-layouts  6.27 us

profile of v1, /device:TPU:2, one launch (start us, length us, event | category | flops | bytes accessed | tf_op | source)
XLA Modules:
  0.0 87.6 jit_solution(4165063251344406580)
XLA Ops:
  0.6 0.0 copy-start
  0.6 1.0 %copy-done = f32[512,256]{1,0:T(8,128)S(1)} copy-done((f32[512,256]{1,0:T(8,128)S(1)}, f32[512,256]{1,0:T(8,128)}, u32[]{:S(2)}) %copy-start) | copy-done | bytes 524312
  1.7 0.0 copy-start.1
  1.7 1.0 %copy-done.1 = f32[512,256]{1,0:T(8,128)S(1)} copy-done((f32[512,256]{1,0:T(8,128)S(1)}, f32[512,256]{1,0:T(8,128)}, u32[]{:S(2)}) %copy-start.1) | copy-done | bytes 524312
  2.7 0.0 copy-start.2
  2.7 0.9 %copy-done.2 = bf16[512,256]{1,0:T(8,128)(2,1)S(1)} copy-done((bf16[512,256]{1,0:T(8,128)(2,1)S(1)}, bf16[512,256]{1,0:T(8,128)(2,1)}, u32[]{:S(2)}) %copy-start.2) | copy-done | bytes 262168
  3.7 0.0 copy-start.3
  3.7 0.9 %copy-done.3 = f32[256,256]{1,0:T(8,128)S(1)} copy-done((f32[256,256]{1,0:T(8,128)S(1)}, f32[256,256]{1,0:T(8,128)}, u32[]{:S(2)}) %copy-start.3) | copy-done | bytes 262168
  4.6 80.7 %dion_step.1 = (f32[512,256]{1,0:T(8,128)S(1)}, f32[512,256]{1,0:T(8,128)S(1)}, f32[256,256]{1,0:T(8,128)S(1)}) custom-call(f32[512,256]{1,0:T(8,128)S(1)} %copy-done, f32[512,256]{1,0:T(8,128)S(1)} %copy-done.1, bf16[512,256]{1,0:T(8,128)(2,1)S(1)} %copy-done.2, f32[256,256]{1,0:T(8,128)S(1)} %copy-done.3), custom_call_target="tpu_custom_call" | custom-call | tf_op jit(solution)/shard_map/dion_step/pallas_call | solution.py:289
  85.3 0.8 copy.10
  86.1 0.8 copy.11
  86.9 0.7 copy.12
Async XLA Ops:
  0.6 1.0 %copy-start = (f32[512,256]{1,0:T(8,128)S(1)}, f32[512,256]{1,0:T(8,128)}, u32[]{:S(2)}) copy-start(f32[512,256]{1,0:T(8,128)} %weight_hbm.1) | copy-start | bytes 1572868
  1.7 1.0 %copy-start.1 = (f32[512,256]{1,0:T(8,128)S(1)}, f32[512,256]{1,0:T(8,128)}, u32[]{:S(2)}) copy-start(f32[512,256]{1,0:T(8,128)} %momentum_hbm.1) | copy-start | bytes 1572868
  2.7 0.9 %copy-start.2 = (bf16[512,256]{1,0:T(8,128)(2,1)S(1)}, bf16[512,256]{1,0:T(8,128)(2,1)}, u32[]{:S(2)}) copy-start(bf16[512,256]{1,0:T(8,128)(2,1)} %gradient_hbm.1) | copy-start | bytes 786436
  3.7 0.9 %copy-start.3 = (f32[256,256]{1,0:T(8,128)S(1)}, f32[256,256]{1,0:T(8,128)}, u32[]{:S(2)}) copy-start(f32[256,256]{1,0:T(8,128)} %factor_hbm.1) | copy-start | bytes 786436

commit v2 on v1

v2 whole, which is shorter than its diff:
```python
import functools
import math

import jax
import jax.numpy as jnp
from jax import lax
from jax.experimental import pallas as pl
from jax.experimental.pallas import tpu as pltpu
from jax.sharding import PartitionSpec as P

D_IN = 16384
RANK = 256
LANES = 128
MESH = pl.DeviceIdType.MESH
F32 = jnp.float32

FAR_X, NEAR_X, FAR_Z, NEAR_Z, IN_X, IN_Z, BACK_X, BACK_Z = 0, 1, 2, 3, 4, 5, 6, 9
ALL_X, ALL_Z, GRAM, GRAM_FIRST, GRAM_REST, RIGHT, RIGHT_ALL, SQUARES, BATCHES = range(12, 21)


def dot(first, second, first_dim, second_dim):
    return lax.dot_general(
        first,
        second,
        (((first_dim,), (second_dim,)), ((), ())),
        precision=lax.Precision.HIGHEST,
        preferred_element_type=F32,
    )


def iota(shape, dim):
    return lax.broadcasted_iota(jnp.int32, shape, dim)


def inverse_factor(work, block, inner, fill_rest):
    n = work.shape[0]

    def step(index, carry):
        panel = work[0:block, :]
        lane = iota((block, n), 1)
        sub = iota((block, n), 0)
        narrow = iota((block, LANES), 0)
        row_lane = iota((1, n), 1)
        for start in range(0, block, inner):
            columns = [
                jnp.broadcast_to(panel[:, start + j : start + j + 1], (block, LANES)) for j in range(inner)
            ]
            for j in range(inner):
                k = start + j
                scale = lax.rsqrt(columns[j][k : k + 1, :])
                factor = jnp.where(narrow > k, columns[j] * scale, 0.0)
                row = jnp.where(row_lane == k, 1.0, panel[k : k + 1, :])
                row = row * jnp.concatenate([scale] * (n // LANES), axis=1)
                for later in range(j + 1, inner):
                    columns[later] = columns[later] - factor * (columns[later][k : k + 1, :] * scale)
                wide = jnp.concatenate([factor] * (n // LANES), axis=1)
                below = jnp.where((lane == k) & (sub > k), 0.0, panel) - wide * row
                panel = jnp.where(sub == k, jnp.broadcast_to(row, (block, n)), below)
        pl.when(index == 0)(fill_rest)
        left = n - block * index
        own = jnp.where((lane > sub) & (lane < left), 0.0, panel)
        right_side = jnp.where((lane < block) & (lane > sub), 0.0, panel)
        left_side = jnp.where((lane < left) & (lane >= block), panel, 0.0)
        update = dot(left_side[:, block:], right_side, 0, 0)
        rest_lane = iota((n - block, n), 1)
        rest_sub = iota((n - block, n), 0) + block
        rest = jnp.where((rest_lane < block) & (rest_sub < left), 0.0, work[block:, :]) - update
        work[0 : n - block, :] = pltpu.roll(rest, n - block, 1)
        work[n - block :, :] = pltpu.roll(own, n - block, 1)
        return carry

    lax.fori_loop(0, n // block, step, 0)


def kernel(
    side, depth, weight_hbm, momentum_hbm, gradient_hbm, factor_hbm,
    weight, new_momentum, left_factor, right_raw, total,
    momentum, gradient, factor, combined, product, partial, scatter_in, middle, middle_in, gathered, left, gram, gram_in,
    gram_all, work, right, right_in, right_all, squares, squares_in, load_sem, send_sem, recv_sem,
):
    col, row = lax.axis_index("col"), lax.axis_index("row")
    z, x = lax.div(col, side), lax.rem(col, side)
    here, half = (x, z), side // 2
    far = sorted(range(1, side), key=lambda k: -min(k, side - k))
    far_row = sorted(range(1, 2 * depth), key=lambda k: -min(k // 2, depth - k // 2))

    def x_peer(k):
        return at(z, lax.rem(x + k, side))

    def z_peer(k):
        return at(lax.rem(z + k, side), x)

    def at(z_of, x_of):
        return (z_of * side + x_of, row)

    def row_peer(k):
        return lax.rem(row + k, 2 * depth)

    def send(source, target, batch, device):
        pltpu.make_async_remote_copy(
            src_ref=source,
            dst_ref=target,
            send_sem=send_sem.at[batch],
            recv_sem=recv_sem.at[batch],
            device_id=device,
            device_id_type=MESH,
        ).start()

    def arrived(target, batch):
        pltpu.make_async_copy(target, target, recv_sem.at[batch]).wait()

    def sent(source, batch):
        pltpu.make_async_copy(source, source, send_sem.at[batch]).wait()

    barrier = pltpu.get_barrier_semaphore()
    for k in far:
        pl.semaphore_signal(barrier, inc=1, device_id=x_peer(k), device_id_type=MESH)
        pl.semaphore_signal(barrier, inc=1, device_id=z_peer(k), device_id_type=MESH)
    for k in far_row:
        pl.semaphore_signal(barrier, inc=1, device_id=(col, row_peer(k)), device_id_type=MESH)

    loads = [
        pltpu.make_async_copy(source, target, load_sem.at[i])
        for i, (source, target) in enumerate(
            ((momentum_hbm, momentum), (gradient_hbm, gradient), (factor_hbm, factor), (weight_hbm, weight))
        )
    ]
    for load in loads:
        load.start()
    for load in loads[:3]:
        load.wait()
    combined[...] = momentum[...] + gradient[...].astype(F32)
    whole = dot(combined[...], factor[...], 1, 0)
    tiles = product.shape[1:]
    product[0] = whole[:, :LANES].reshape(tiles)
    product[1] = whole[:, LANES:].reshape(tiles)

    def place(part, o):
        return lax.rem(here[1 - part] + o + side - 1, side)

    for o in range(side):
        partial[0, :, o] = product[0, :, place(0, o)]
        partial[1, o] = product[1, place(1, o)]

    pl.semaphore_wait(barrier, 2 * len(far) + len(far_row))

    def scatter(low, batch_x, batch_z):
        tiles = pl.ds(low, half)
        for k in far:
            send(partial.at[0, lax.rem(x + k, side), tiles], scatter_in.at[0, k, tiles], batch_x, x_peer(k))
            send(partial.at[1, tiles, lax.rem(z + k, side)], scatter_in.at[1, k, tiles], batch_z, z_peer(k))

    def reduce_on(low, part, batch):
        tiles = pl.ds(low, half)
        arrived(scatter_in.at[part, pl.ds(1, side - 1), tiles], batch)
        own = partial[0, x, tiles] if part == 0 else partial[1, tiles, z]
        middle[part, tiles] = own + jnp.sum(scatter_in[part, 1:, tiles], axis=0)
        peer, onward = (z_peer, IN_Z) if part == 0 else (x_peer, IN_X)
        for k in far:
            o = (k + 1) % side
            if low <= o < low + half:
                send(middle.at[part, o], middle_in.at[part, k], onward, peer(k))

    scatter(half, FAR_X, FAR_Z)
    scatter(0, NEAR_X, NEAR_Z)
    reduce_on(half, 0, FAR_X)
    reduce_on(half, 1, FAR_Z)
    reduce_on(0, 0, NEAR_X)
    reduce_on(0, 1, NEAR_Z)

    groups = [(0, min(3, side)), (min(3, side), half + 1), (half + 1, side)]
    groups = [(low, high) for low, high in groups if high > low]

    def group_of(o):
        return next(g for g, (low, high) in enumerate(groups) if low <= o < high)

    def count(g):
        return sum(1 for o in range(*groups[g]) if o != 1)

    for part, batch, back, peer in ((0, IN_Z, BACK_Z, z_peer), (1, IN_X, BACK_X, x_peer)):
        arrived(middle_in.at[part, pl.ds(1, side - 1)], batch)
        gathered[part, here[part], 1] = middle[part, 1] + jnp.sum(middle_in[part, 1:], axis=0)
        for k in far:
            o = (1 - k) % side
            send(
                gathered.at[part, here[part], 1], gathered.at[part, here[part], o], back + group_of(o), peer(k)
            )
    for g, (low, high) in enumerate(groups):
        for part, back, batch, peer in ((0, BACK_Z, ALL_X, x_peer), (1, BACK_X, ALL_Z, z_peer)):
            if count(g):
                arrived(middle_in.at[part, pl.ds(0, count(g))], back + g)
            block = gathered.at[part, here[part], pl.ds(low, high - low)]
            for k in far:
                send(block, block, batch, peer(k))
    arrived(gathered.at[0, pl.ds(1, side - 1)], ALL_X)
    arrived(gathered.at[1, pl.ds(1, side - 1)], ALL_Z)
    for o in range(side):
        left[0, :, place(0, o)] = gathered[0, :, o]
        left[1, place(1, o)] = gathered[1, :, o]

    rows = combined.shape[0]
    halves = [left[part].reshape(rows, LANES) for part in range(2)]
    left_raw = jnp.concatenate(halves, axis=1)
    tile_rows = 2 * RANK // (side * side)
    tile = pl.ds(col * tile_rows, tile_rows)
    start = col * tile_rows
    block_row = lax.rem(lax.div(start, LANES), 2)
    block_col = lax.div(start, RANK)
    gram[...] = dot(left[block_row].reshape(rows, LANES), left[block_col].reshape(rows, LANES), 0, 0)
    own_tile = pl.ds(lax.rem(start, LANES), tile_rows)
    gram_in[row] = gram[own_tile]
    for k in far_row:
        send(gram.at[own_tile], gram_in.at[row], GRAM, (col, row_peer(k)))

    right[...] = dot(combined[...], left_raw, 0, 0)
    strip_rows = RANK // (2 * depth)
    strip = pl.ds(row * strip_rows, strip_rows)
    for k in far_row:
        send(right.at[pl.ds(row_peer(k) * strip_rows, strip_rows)], right_in.at[k], RIGHT, (col, row_peer(k)))

    arrived(gram_in.at[pl.ds(0, 2 * depth - 1)], GRAM)
    gram_in[0] = jnp.sum(gram_in[...], axis=0)

    def plane(start):
        def one(j, carry):
            dz, dx = far_of(lax.div(j, side)), far_of(lax.rem(j, side))
            start(at(lax.rem(z + dz, side), lax.rem(x + dx, side)))
            return carry

        lax.fori_loop(0, side * side - 1, one, 0)

    def far_of(j):
        step = lax.div(j + 1, 2)
        return half + jnp.where(lax.rem(j, 2) == 1, -step, step)

    panel_rows = RANK // 4
    first = lax.rem(start, RANK) < panel_rows
    gram_batch = jnp.where(first, GRAM_FIRST, GRAM_REST)
    plane(lambda device: send(gram_in.at[0], gram_all.at[tile], gram_batch, device))
    pltpu.make_async_copy(gram_in.at[0], gram_all.at[tile], recv_sem.at[gram_batch]).start()

    arrived(right_in.at[pl.ds(1, 2 * depth - 1)], RIGHT)
    right_all[strip] = right[strip] + jnp.sum(right_in[1:], axis=0)
    for k in far_row:
        send(right_all.at[strip], right_all.at[strip], RIGHT_ALL, (col, row_peer(k)))

    def fill(low, size):
        work[pl.ds(low, size), :LANES] = gram_all[pl.ds(low, size)]
        work[pl.ds(low, size), LANES:] = gram_all[pl.ds(RANK + low, size)]

    def fill_rest():
        arrived(gram_all.at[pl.ds(0, 2 * (RANK - panel_rows))], GRAM_REST)
        fill(panel_rows, RANK - panel_rows)

    arrived(gram_all.at[pl.ds(0, 2 * panel_rows)], GRAM_FIRST)
    fill(0, panel_rows)
    inverse_factor(work, panel_rows, 16, fill_rest)
    inverse = work[...]

    arrived(right_all.at[pl.ds(0, RANK - strip_rows)], RIGHT_ALL)
    raw = dot(right_all[...], inverse, 1, 1)
    sums = jnp.sum(raw * raw, axis=0, keepdims=True)
    squares[0:1] = sums[:, :LANES]
    squares[1:2] = sums[:, LANES:]
    squares_in[col] = squares[...]
    plane(lambda device: send(squares, squares_in.at[col], SQUARES, device))

    right_raw[...] = raw
    left_factor[...] = dot(left_raw, inverse, 1, 1)
    new_momentum[...] = combined[...] - 0.05 * dot(left_factor[...], raw, 1, 1)
    loads[3].wait()

    sent(scatter_in.at[0, pl.ds(1, side - 1), pl.ds(0, half)], FAR_X)
    sent(scatter_in.at[0, pl.ds(1, side - 1), pl.ds(0, half)], NEAR_X)
    sent(scatter_in.at[1, pl.ds(1, side - 1), pl.ds(0, half)], FAR_Z)
    sent(scatter_in.at[1, pl.ds(1, side - 1), pl.ds(0, half)], NEAR_Z)
    sent(middle_in.at[0, pl.ds(1, side - 1)], IN_Z)
    sent(middle_in.at[1, pl.ds(1, side - 1)], IN_X)
    for g in range(len(groups)):
        if count(g):
            sent(middle_in.at[0, pl.ds(0, count(g))], BACK_Z + g)
            sent(middle_in.at[1, pl.ds(0, count(g))], BACK_X + g)
    sent(gathered.at[0, pl.ds(1, side - 1)], ALL_X)
    sent(gathered.at[1, pl.ds(1, side - 1)], ALL_Z)
    sent(gram_in.at[pl.ds(0, 2 * depth - 1)], GRAM)
    sent(gram_all.at[pl.ds(0, 2 * RANK - tile_rows)], gram_batch)
    sent(right_in.at[pl.ds(1, 2 * depth - 1)], RIGHT)
    sent(right_all.at[pl.ds(0, RANK - strip_rows)], RIGHT_ALL)

    arrived(squares_in.at[pl.ds(0, side * side - 1)], SQUARES)
    total[...] = jnp.sum(squares_in[...], axis=0)
    sent(squares_in.at[pl.ds(0, side * side - 1)], SQUARES)


def finish(
    weight, momentum_now, left_factor, right_raw, total, new_weight_hbm, new_momentum_hbm, new_factor_hbm,
    new_weight, new_factor, store_sem,
):
    store_momentum = pltpu.make_async_copy(momentum_now, new_momentum_hbm, store_sem.at[0])
    store_momentum.start()
    sums = jnp.concatenate([total[0:1], total[1:2]], axis=1)
    new_factor[...] = right_raw[...] / jnp.sqrt(sums / D_IN + 1e-06)
    store_factor = pltpu.make_async_copy(new_factor, new_factor_hbm, store_sem.at[1])
    store_factor.start()
    parts = 2
    size = weight.shape[0] // parts
    stores = []
    for part in range(parts):
        block = pl.ds(part * size, size)
        new_weight[block] = weight[block] - 0.5 * dot(left_factor[block], new_factor[...], 1, 1)
        stores.append(
            pltpu.make_async_copy(new_weight.at[block], new_weight_hbm.at[block], store_sem.at[2 + part])
        )
        stores[-1].start()
    store_momentum.wait()
    store_factor.wait()
    for store in stores:
        store.wait()


def on_device(side, depth, weight, momentum, gradient, right_factor):
    rows, columns = weight.shape
    small = rows // side // side
    tile_rows = 2 * RANK // (side * side)
    vmem = pltpu.VMEM
    tiles = (side, side, small, LANES)
    big = jax.ShapeDtypeStruct((rows, columns), F32)
    tall = jax.ShapeDtypeStruct((rows, RANK), F32)
    square = jax.ShapeDtypeStruct((columns, RANK), F32)
    scratch = [
        vmem((rows, columns), F32),
        vmem((rows, columns), gradient.dtype),
        vmem((columns, RANK), F32),
        vmem((rows, columns), F32),
        vmem((2, *tiles), F32),
        vmem((2, *tiles), F32),
        vmem((2, *tiles), F32),
        vmem((2, side, small, LANES), F32),
        vmem((2, side, small, LANES), F32),
        vmem((2, *tiles), F32),
        vmem((2, *tiles), F32),
        vmem((LANES, LANES), F32),
        vmem((2 * depth, tile_rows, LANES), F32),
        vmem((2 * RANK, LANES), F32),
        vmem((RANK, RANK), F32),
        vmem((columns, RANK), F32),
        vmem((2 * depth, columns // (2 * depth), RANK), F32),
        vmem((columns, RANK), F32),
        vmem((2, LANES), F32),
        vmem((side * side, 2, LANES), F32),
        pltpu.SemaphoreType.DMA((4,)),
        pltpu.SemaphoreType.DMA((BATCHES,)),
        pltpu.SemaphoreType.DMA((BATCHES,)),
    ]
    arguments = [pltpu.with_memory_space_constraint(a, pltpu.HBM) for a in (weight, momentum, gradient, right_factor)]
    middle = pl.pallas_call(
        functools.partial(kernel, side, depth),
        out_shape=(big, big, tall, square, jax.ShapeDtypeStruct((2, LANES), F32)),
        in_specs=[pl.BlockSpec(memory_space=pl.ANY)] * 4,
        out_specs=(pl.BlockSpec(memory_space=vmem),) * 5,
        scratch_shapes=scratch,
        compiler_params=pltpu.CompilerParams(
            collective_id=0, has_side_effects=True, vmem_limit_bytes=24 * 1024 * 1024
        ),
        name="dion_step",
    )(*arguments)
    return pl.pallas_call(
        finish,
        out_shape=(big, big, square),
        in_specs=[pl.BlockSpec(memory_space=vmem)] * 5,
        out_specs=(pl.BlockSpec(memory_space=pl.ANY),) * 3,
        scratch_shapes=[vmem((rows, columns), F32), vmem((columns, RANK), F32), pltpu.SemaphoreType.DMA((4,))],
        compiler_params=pltpu.CompilerParams(vmem_limit_bytes=24 * 1024 * 1024),
        name="dion_finish",
    )(*middle)


def solution(mesh):
    side = math.isqrt(mesh.shape["col"])
    depth = mesh.shape["row"] // 2
    in_specs = (P("row", "col"), P("row", "col"), P("row", "col"), P("col", None))
    out_specs = (P("row", "col"), P("row", "col"), P("col", None))
    return jax.shard_map(
        functools.partial(on_device, side, depth), mesh=mesh, in_specs=in_specs, out_specs=out_specs, check_vma=False
    )
```

time: 87.9 us -> 77.6 us (0.88)
  local copies, waits for them, and re-layouts: 6.27 us -> 0 us
  Pallas kernels: 80.7 us -> 76.8 us
    unnamed x11 -> x0, local copies, waits for them, and re-layouts: 6.27 us -> none
    pallas_call x1 -> x2, Pallas kernels: 80.7 us -> 76.8 us  [the longest x1 75.3 us: on_device(): pl.pallas_call(functools.partial(kernel, side, depth), out_shape=(big, bi...]
where the time goes in v2:
time: 77.6 us; the launch traced here: 77.4 us
  Pallas kernels  76.8 us (99%)
    pallas_call x1, Pallas kernels, on_device(): pl.pallas_call(functools.partial(kernel, side, depth), out_shape=(big, bi...  75.3 us

profile of v2, /device:TPU:2, one launch (start us, length us, event | category | flops | bytes accessed | tf_op | source)
XLA Modules:
  0.0 77.4 jit_solution(17178592611755481689)
XLA Ops:
  0.6 75.3 %dion_step.1 = (f32[512,256]{1,0:T(8,128)S(1)}, f32[512,256]{1,0:T(8,128)S(1)}, f32[512,256]{1,0:T(8,128)S(1)}, f32[256,256]{1,0:T(8,128)S(1)}, f32[2,128]{1,0:T(2,128)S(1)}) custom-call(f32[512,256]{1,0:T(8,128)} %weight_hbm.1, f32[512,256]{1,0:T(8,128)} %momentum_hbm.1, bf16[512,256]{1,0:T(8,128)(2,1)} %gradient_hbm.1, f32[256,256]{1,0:T(8,128)} %factor_hbm.1), custom_call_target="tpu_custom_call" | custom-call | tf_op jit(solution)/shard_map/dion_step/pallas_call | solution.py:356
  75.9 1.5 %dion_finish.1 = (f32[512,256]{1,0:T(8,128)}, f32[512,256]{1,0:T(8,128)}, f32[256,256]{1,0:T(8,128)}) custom-call(f32[512,256]{1,0:T(8,128)S(1)} %get-tuple-element.8.weight, f32[512,256]{1,0:T(8,128)S(1)} %get-tuple-element.9.momentum_now, f32[512,256]{1,0:T(8,128)S(1)} %get-tuple-element.10.left_factor, f32[256,256]{1,0:T(8,128)S(1)} %get-tuple-element.11.right_raw, ...), custom_call_target="tpu_custom_call" | custom-call | tf_op jit(solution)/shard_map/dion_finish/pallas_call | solution.py:367

commit v3 on v2

v3 whole, which is shorter than its diff:
```python
import functools
import math

import jax
import jax.numpy as jnp
from jax import lax
from jax.experimental import pallas as pl
from jax.experimental.pallas import tpu as pltpu
from jax.sharding import PartitionSpec as P

D_IN = 16384
RANK = 256
LANES = 128
MESH = pl.DeviceIdType.MESH
F32 = jnp.float32

OUT_X, OUT_Z, BACK_X, BACK_Z = 0, 4, 8, 12
IN_X, IN_Z, ALL_X, ALL_Z, GRAM, GRAM_FIRST, GRAM_REST, PAIR, RIGHT, RIGHT_ALL, SQUARES, BATCHES = range(16, 28)


def dot(first, second, first_dim, second_dim):
    return lax.dot_general(
        first,
        second,
        (((first_dim,), (second_dim,)), ((), ())),
        precision=lax.Precision.HIGHEST,
        preferred_element_type=F32,
    )


def iota(shape, dim):
    return lax.broadcasted_iota(jnp.int32, shape, dim)


def eliminate(panel, first, inner):
    block, n = panel.shape
    copies = n // LANES

    def spread(column, r):
        return jnp.broadcast_to(column[r // 8, r % 8 : r % 8 + 1, :], (8, LANES))

    done = []
    for start in range(0, block, inner):
        rows = panel.shape[0]
        low = first + start
        columns = [
            jnp.broadcast_to(panel[:, low + j : low + j + 1], (rows, LANES)).reshape(rows // 8, 8, LANES)
            for j in range(inner)
        ]
        lane, sub = iota((rows, n), 1), iota((rows, n), 0)
        identity = jnp.where(lane - low == sub, 1.0, 0.0)
        panel = jnp.where((lane >= low) & (lane < low + inner), identity, panel)
        pivot = spread(columns[0], 0)
        scales, dropped = [], 0
        for j in range(inner):
            r = j - dropped
            scale = lax.rsqrt(pivot)
            scales.append(scale[:1])
            if j + 1 < inner:
                side = spread(columns[j], r + 1) * scale
                pivot = spread(columns[j + 1], r + 1) - side * side
            scaled = columns[j] * scale[None]
            for later in range(j + 1, inner):
                columns[later] = columns[later] - scaled * (spread(columns[later], r) * scale)[None]
            live = panel.shape[0]
            factor = (scaled * scale[None]).reshape(live, LANES)
            factor = jnp.where(iota((live, LANES), 0) > r, factor, 0.0)
            factor = jnp.concatenate([factor] * copies, axis=1)
            panel = panel - factor * jnp.broadcast_to(panel[r : r + 1, :], (live, n))
            if r == 7:
                all_scales = jnp.concatenate(scales, axis=0)
                done.append(panel[:8] * jnp.concatenate([all_scales] * copies, axis=1))
                panel = panel[8:]
                columns = [c[1:] if i > j else c for i, c in enumerate(columns)]
                scales, dropped = [], dropped + 8
    return jnp.concatenate(done, axis=0)


def inverse_factor(work, fill_rest):
    n = work.shape[0]
    half, block = n // 2, n // 4

    def swapped(value):
        return jnp.concatenate([value[:, half:], value[:, :half]], axis=1)

    def step(index, carry):
        lane, sub = iota((block, n), 1), iota((block, n), 0)
        upper = eliminate(work[0:block, :], 0, 16)
        pl.when(index == 0)(fill_rest)
        own_part = jnp.where((lane < block) & (lane > sub), 0.0, upper)
        lower = jnp.where(lane < block, 0.0, work[block:half, :]) - dot(upper[:, block:half], own_part, 0, 0)
        lower = eliminate(lower, block, 16)
        both = jnp.concatenate([upper, lower], axis=0)
        lane, sub = iota((half, n), 1), iota((half, n), 0)
        ready = swapped(jnp.where((lane > sub) & (lane < n - half * index), 0.0, both))

        @pl.when(index == 0)
        def _():
            own_part = jnp.where((lane < half) & (lane > sub), 0.0, both)
            rest = jnp.where(lane < half, 0.0, work[half:, :]) - dot(both[:, half:], own_part, 0, 0)
            work[0:half, :] = swapped(rest)

        @pl.when(index == 1)
        def _():
            work[0:half, :] = swapped(work[half:, :])

        work[half:, :] = ready
        return carry

    lax.fori_loop(0, 2, step, 0)


def kernel(
    side, depth, weight_hbm, momentum_hbm, gradient_hbm, factor_hbm,
    weight, new_momentum, left_factor, right_raw, total,
    momentum, gradient, factor, combined, product, partial, scatter_in, middle, middle_in, gathered, left, gram, gram_in,
    gram_all, work, right, pair_in, right_in, right_all, squares, squares_in, load_sem, send_sem, recv_sem,
):
    col, row = lax.axis_index("col"), lax.axis_index("row")
    z, x = lax.div(col, side), lax.rem(col, side)
    here, half = (x, z), side // 2
    offsets = sorted(range(side), key=lambda k: min(k, side - k))
    groups = [
        [slot for slot, k in enumerate(offsets) if min(k, side - k, 3) == distance] for distance in range(4)
    ]
    groups = [(slots[0], len(slots)) for slots in groups if slots]
    far = sorted(range(1, side), key=lambda k: -min(k, side - k))
    far_row = sorted(range(1, 2 * depth), key=lambda k: -min(k // 2, depth - k // 2))

    def x_peer(k):
        return at(z, lax.rem(x + k, side))

    def z_peer(k):
        return at(lax.rem(z + k, side), x)

    def at(z_of, x_of):
        return (z_of * side + x_of, row)

    def row_peer(k):
        return lax.rem(row + k, 2 * depth)

    def send(source, target, batch, device):
        pltpu.make_async_remote_copy(
            src_ref=source,
            dst_ref=target,
            send_sem=send_sem.at[batch],
            recv_sem=recv_sem.at[batch],
            device_id=device,
            device_id_type=MESH,
        ).start()

    def arrived(target, batch):
        pltpu.make_async_copy(target, target, recv_sem.at[batch]).wait()

    def sent(source, batch):
        pltpu.make_async_copy(source, source, send_sem.at[batch]).wait()

    barrier = pltpu.get_barrier_semaphore()
    for k in far:
        pl.semaphore_signal(barrier, inc=1, device_id=x_peer(k), device_id_type=MESH)
        pl.semaphore_signal(barrier, inc=1, device_id=z_peer(k), device_id_type=MESH)
    for k in far_row:
        pl.semaphore_signal(barrier, inc=1, device_id=(col, row_peer(k)), device_id_type=MESH)

    loads = [
        pltpu.make_async_copy(source, target, load_sem.at[i])
        for i, (source, target) in enumerate(
            ((momentum_hbm, momentum), (gradient_hbm, gradient), (factor_hbm, factor), (weight_hbm, weight))
        )
    ]
    for load in loads:
        load.start()
    for load in loads[:3]:
        load.wait()
    combined[...] = momentum[...] + gradient[...].astype(F32)
    whole = dot(combined[...], factor[...], 1, 0)
    tiles = product.shape[1:]
    product[0] = whole[:, :LANES].reshape(tiles)
    product[1] = whole[:, LANES:].reshape(tiles)

    def place(part, slot):
        return lax.rem(here[1 - part] + offsets[slot], side)

    for slot in range(side):
        partial[0, :, slot] = product[0, :, place(0, slot)]
        partial[1, slot] = product[1, place(1, slot)]

    pl.semaphore_wait(barrier, 2 * len(far) + len(far_row))

    for g, (low, size) in reversed(list(enumerate(groups))):
        tiles = pl.ds(low, size)
        for k in far:
            send(partial.at[0, lax.rem(x + k, side), tiles], scatter_in.at[0, k, tiles], OUT_X + g, x_peer(k))
            send(partial.at[1, tiles, lax.rem(z + k, side)], scatter_in.at[1, k, tiles], OUT_Z + g, z_peer(k))
    for g, (low, size) in reversed(list(enumerate(groups))):
        tiles = pl.ds(low, size)
        for part, batch, onward, peer in ((0, OUT_X, IN_Z, z_peer), (1, OUT_Z, IN_X, x_peer)):
            arrived(scatter_in.at[part, pl.ds(1, side - 1), tiles], batch + g)
            own = partial[0, x, tiles] if part == 0 else partial[1, tiles, z]
            middle[part, tiles] = own + jnp.sum(scatter_in[part, 1:, tiles], axis=0)
            for slot in reversed(range(low, low + size)):
                k = offsets[slot]
                if k:
                    send(middle.at[part, slot], middle_in.at[part, k], onward, peer(k))

    def forward(g, part):
        batch, peer = ((ALL_X, x_peer), (ALL_Z, z_peer))[part]
        block = gathered.at[part, here[part], pl.ds(*groups[g])]
        for k in far:
            send(block, block, batch, peer(k))

    group_of = [g for g, (low, size) in enumerate(groups) for _ in range(size)]
    for part, batch, back, peer in ((0, IN_Z, BACK_Z, z_peer), (1, IN_X, BACK_X, x_peer)):
        arrived(middle_in.at[part, pl.ds(1, side - 1)], batch)
        own = gathered.at[part, here[part], 0]
        own[...] = middle[part, 0] + jnp.sum(middle_in[part, 1:], axis=0)
        for k in far:
            slot = offsets.index(side - k)
            send(own, gathered.at[part, here[part], slot], back + group_of[slot], peer(k))
        forward(0, part)
    for g in range(1, len(groups)):
        for part, back in ((0, BACK_Z), (1, BACK_X)):
            arrived(middle_in.at[part, pl.ds(0, groups[g][1])], back + g)
            forward(g, part)
    arrived(gathered.at[0, pl.ds(1, side - 1)], ALL_X)
    arrived(gathered.at[1, pl.ds(1, side - 1)], ALL_Z)
    for slot in range(side):
        left[0, :, place(0, slot)] = gathered[0, :, slot]
        left[1, place(1, slot)] = gathered[1, :, slot]

    rows = combined.shape[0]
    halves = [left[part].reshape(rows, LANES) for part in range(2)]
    left_raw = jnp.concatenate(halves, axis=1)
    tile_rows = 2 * RANK // (side * side)
    tile = pl.ds(col * tile_rows, tile_rows)
    start = col * tile_rows
    block_row = lax.rem(lax.div(start, LANES), 2)
    block_col = lax.div(start, RANK)
    gram[...] = dot(left[block_row].reshape(rows, LANES), left[block_col].reshape(rows, LANES), 0, 0)
    own_tile = pl.ds(lax.rem(start, LANES), tile_rows)
    gram_in[row] = gram[own_tile]
    used = (block_row == 0) | (block_col == 1)

    @pl.when(used)
    def _():
        for k in far_row:
            send(gram.at[own_tile], gram_in.at[row], GRAM, (col, row_peer(k)))

    core, y = lax.rem(row, 2), lax.div(row, 2)
    pair_rows = RANK // 2
    right[...] = dot(combined[...], left_raw, 0, 0)
    send(right.at[pl.ds((1 - core) * pair_rows, pair_rows)], pair_in, PAIR, (col, row + 1 - 2 * core))
    arrived(pair_in, PAIR)
    mine = pl.ds(core * pair_rows, pair_rows)
    right[mine] = right[mine] + pair_in[...]

    strip_rows = pair_rows // depth

    def strip_of(y_of):
        return pl.ds(core * pair_rows + y_of * strip_rows, strip_rows)

    for k in sorted(range(1, depth), key=lambda k: -min(k, depth - k)):
        y_peer = lax.rem(y + k, depth)
        send(right.at[strip_of(y_peer)], right_in.at[k], RIGHT, (col, 2 * y_peer + core))

    def plane(start):
        def one(j, carry):
            dz, dx = far_of(lax.div(j, side)), far_of(lax.rem(j, side))
            start(at(lax.rem(z + dz, side), lax.rem(x + dx, side)))
            return carry

        lax.fori_loop(0, side * side - 1, one, 0)

    def far_of(j):
        step = lax.div(j + 1, 2)
        return half + jnp.where(lax.rem(j, 2) == 1, -step, step)

    panel_rows = RANK // 4
    first = lax.rem(start, RANK) < panel_rows
    gram_batch = jnp.where(first, GRAM_FIRST, GRAM_REST)

    @pl.when(used)
    def _():
        arrived(gram_in.at[pl.ds(0, 2 * depth - 1)], GRAM)
        gram_in[0] = jnp.sum(gram_in[...], axis=0)
        plane(lambda device: send(gram_in.at[0], gram_all.at[tile], gram_batch, device))
        pltpu.make_async_copy(gram_in.at[0], gram_all.at[tile], recv_sem.at[gram_batch]).start()

    strip = strip_of(y)
    if depth > 1:
        arrived(right_in.at[pl.ds(1, depth - 1)], RIGHT)
    right_all[strip] = right[strip] + jnp.sum(right_in[1:], axis=0)
    for k in far_row:
        send(right_all.at[strip], right_all.at[strip], RIGHT_ALL, (col, row_peer(k)))

    def fill_rest():
        arrived(gram_all.at[pl.ds(0, 2 * (RANK - panel_rows) - LANES)], GRAM_REST)
        work[panel_rows:LANES, :LANES] = gram_all[panel_rows:LANES]
        work[panel_rows:, LANES:] = gram_all[RANK + panel_rows :]

    arrived(gram_all.at[pl.ds(0, 2 * panel_rows)], GRAM_FIRST)
    work[0:panel_rows, :LANES] = gram_all[0:panel_rows]
    work[0:panel_rows, LANES:] = gram_all[RANK : RANK + panel_rows]
    work[LANES:, :LANES] = jnp.zeros((RANK - LANES, LANES), F32)
    inverse_factor(work, fill_rest)
    inverse = work[...]

    arrived(right_all.at[pl.ds(0, RANK - strip_rows)], RIGHT_ALL)
    raw = dot(right_all[...], inverse, 1, 1)
    sums = jnp.sum(raw * raw, axis=0, keepdims=True)
    squares[0:1] = sums[:, :LANES]
    squares[1:2] = sums[:, LANES:]
    squares_in[col] = squares[...]
    plane(lambda device: send(squares, squares_in.at[col], SQUARES, device))

    right_raw[...] = raw
    left_factor[...] = dot(left_raw, inverse, 1, 1)
    new_momentum[...] = combined[...] - 0.05 * dot(left_factor[...], raw, 1, 1)
    loads[3].wait()

    for g, (low, size) in enumerate(groups):
        for part, out, back in ((0, OUT_X, BACK_Z), (1, OUT_Z, BACK_X)):
            sent(scatter_in.at[part, pl.ds(1, side - 1), pl.ds(0, size)], out + g)
            if g:
                sent(middle_in.at[part, pl.ds(0, size)], back + g)
    sent(middle_in.at[0, pl.ds(1, side - 1)], IN_Z)
    sent(middle_in.at[1, pl.ds(1, side - 1)], IN_X)
    sent(gathered.at[0, pl.ds(1, side - 1)], ALL_X)
    sent(gathered.at[1, pl.ds(1, side - 1)], ALL_Z)

    @pl.when(used)
    def _():
        sent(gram_in.at[pl.ds(0, 2 * depth - 1)], GRAM)
        sent(gram_all.at[pl.ds(0, 2 * RANK - tile_rows)], gram_batch)

    sent(pair_in, PAIR)
    if depth > 1:
        sent(right_in.at[pl.ds(1, depth - 1)], RIGHT)
    sent(right_all.at[pl.ds(0, RANK - strip_rows)], RIGHT_ALL)

    arrived(squares_in.at[pl.ds(0, side * side - 1)], SQUARES)
    total[...] = jnp.sum(squares_in[...], axis=0)
    sent(squares_in.at[pl.ds(0, side * side - 1)], SQUARES)


def finish(
    weight, momentum_now, left_factor, right_raw, total, new_weight_hbm, new_momentum_hbm, new_factor_hbm,
    new_weight, new_factor, store_sem,
):
    store_momentum = pltpu.make_async_copy(momentum_now, new_momentum_hbm, store_sem.at[0])
    store_momentum.start()
    sums = jnp.concatenate([total[0:1], total[1:2]], axis=1)
    new_factor[...] = right_raw[...] / jnp.sqrt(sums / D_IN + 1e-06)
    store_factor = pltpu.make_async_copy(new_factor, new_factor_hbm, store_sem.at[1])
    store_factor.start()
    parts = 2
    size = weight.shape[0] // parts
    stores = []
    for part in range(parts):
        block = pl.ds(part * size, size)
        new_weight[block] = weight[block] - 0.5 * dot(left_factor[block], new_factor[...], 1, 1)
        stores.append(
            pltpu.make_async_copy(new_weight.at[block], new_weight_hbm.at[block], store_sem.at[2 + part])
        )
        stores[-1].start()
    store_momentum.wait()
    store_factor.wait()
    for store in stores:
        store.wait()


def on_device(side, depth, weight, momentum, gradient, right_factor):
    rows, columns = weight.shape
    small = rows // side // side
    tile_rows = 2 * RANK // (side * side)
    vmem = pltpu.VMEM
    tiles = (side, side, small, LANES)
    big = jax.ShapeDtypeStruct((rows, columns), F32)
    tall = jax.ShapeDtypeStruct((rows, RANK), F32)
    square = jax.ShapeDtypeStruct((columns, RANK), F32)
    scratch = [
        vmem((rows, columns), F32),
        vmem((rows, columns), gradient.dtype),
        vmem((columns, RANK), F32),
        vmem((rows, columns), F32),
        vmem((2, *tiles), F32),
        vmem((2, *tiles), F32),
        vmem((2, *tiles), F32),
        vmem((2, side, small, LANES), F32),
        vmem((2, side, small, LANES), F32),
        vmem((2, *tiles), F32),
        vmem((2, *tiles), F32),
        vmem((LANES, LANES), F32),
        vmem((2 * depth, tile_rows, LANES), F32),
        vmem((2 * RANK, LANES), F32),
        vmem((RANK, RANK), F32),
        vmem((columns, RANK), F32),
        vmem((columns // 2, RANK), F32),
        vmem((depth, columns // (2 * depth), RANK), F32),
        vmem((columns, RANK), F32),
        vmem((2, LANES), F32),
        vmem((side * side, 2, LANES), F32),
        pltpu.SemaphoreType.DMA((4,)),
        pltpu.SemaphoreType.DMA((BATCHES,)),
        pltpu.SemaphoreType.DMA((BATCHES,)),
    ]
    arguments = [pltpu.with_memory_space_constraint(a, pltpu.HBM) for a in (weight, momentum, gradient, right_factor)]
    middle = pl.pallas_call(
        functools.partial(kernel, side, depth),
        out_shape=(big, big, tall, square, jax.ShapeDtypeStruct((2, LANES), F32)),
        in_specs=[pl.BlockSpec(memory_space=pl.ANY)] * 4,
        out_specs=(pl.BlockSpec(memory_space=vmem),) * 5,
        scratch_shapes=scratch,
        compiler_params=pltpu.CompilerParams(
            collective_id=0, has_side_effects=True, vmem_limit_bytes=24 * 1024 * 1024
        ),
        name="dion_step",
    )(*arguments)
    return pl.pallas_call(
        finish,
        out_shape=(big, big, square),
        in_specs=[pl.BlockSpec(memory_space=vmem)] * 5,
        out_specs=(pl.BlockSpec(memory_space=pl.ANY),) * 3,
        scratch_shapes=[vmem((rows, columns), F32), vmem((columns, RANK), F32), pltpu.SemaphoreType.DMA((4,))],
        compiler_params=pltpu.CompilerParams(vmem_limit_bytes=24 * 1024 * 1024),
        name="dion_finish",
    )(*middle)


def solution(mesh):
    side = math.isqrt(mesh.shape["col"])
    depth = mesh.shape["row"] // 2
    in_specs = (P("row", "col"), P("row", "col"), P("row", "col"), P("col", None))
    out_specs = (P("row", "col"), P("row", "col"), P("col", None))
    return jax.shard_map(
        functools.partial(on_device, side, depth), mesh=mesh, in_specs=in_specs, out_specs=out_specs, check_vma=False
    )
```

time: 77.6 us -> 75.6 us (0.974)
  Pallas kernels: 76.8 us -> 74.8 us
    pallas_call x1, Pallas kernels: 75.3 us -> 73.3 us  [on_device(): pl.pallas_call(functools.partial(kernel, side, depth), out_shape=(big, bi...]
where the time goes in v3:
time: 75.6 us; the launch traced here: 75.4 us
  Pallas kernels  74.8 us (99%)
    pallas_call x1, Pallas kernels, on_device(): pl.pallas_call(functools.partial(kernel, side, depth), out_shape=(big, bi...  73.3 us

profile of v3, /device:TPU:2, one launch (start us, length us, event | category | flops | bytes accessed | tf_op | source)
XLA Modules:
  0.0 75.4 jit_solution(11945217956685953421)
XLA Ops:
  0.6 73.3 %dion_step.1 = (f32[512,256]{1,0:T(8,128)S(1)}, f32[512,256]{1,0:T(8,128)S(1)}, f32[512,256]{1,0:T(8,128)S(1)}, f32[256,256]{1,0:T(8,128)S(1)}, f32[2,128]{1,0:T(2,128)S(1)}) custom-call(f32[512,256]{1,0:T(8,128)} %weight_hbm.1, f32[512,256]{1,0:T(8,128)} %momentum_hbm.1, bf16[512,256]{1,0:T(8,128)(2,1)} %gradient_hbm.1, f32[256,256]{1,0:T(8,128)} %factor_hbm.1), custom_call_target="tpu_custom_call" | custom-call | tf_op jit(solution)/shard_map/dion_step/pallas_call | solution.py:408
  74.0 1.5 %dion_finish.1 = (f32[512,256]{1,0:T(8,128)}, f32[512,256]{1,0:T(8,128)}, f32[256,256]{1,0:T(8,128)}) custom-call(f32[512,256]{1,0:T(8,128)S(1)} %get-tuple-element.8.weight, f32[512,256]{1,0:T(8,128)S(1)} %get-tuple-element.9.momentum_now, f32[512,256]{1,0:T(8,128)S(1)} %get-tuple-element.10.left_factor, f32[256,256]{1,0:T(8,128)S(1)} %get-tuple-element.11.right_raw, ...), custom_call_target="tpu_custom_call" | custom-call | tf_op jit(solution)/shard_map/dion_finish/pallas_call | solution.py:419

commit v4 on v3

--- a/solution.py
+++ b/solution.py
@@ -156,11 +156,10 @@
         pltpu.make_async_copy(source, source, send_sem.at[batch]).wait()
 
     barrier = pltpu.get_barrier_semaphore()
-    for k in far:
-        pl.semaphore_signal(barrier, inc=1, device_id=x_peer(k), device_id_type=MESH)
-        pl.semaphore_signal(barrier, inc=1, device_id=z_peer(k), device_id_type=MESH)
-    for k in far_row:
-        pl.semaphore_signal(barrier, inc=1, device_id=(col, row_peer(k)), device_id_type=MESH)
+    greeted = [(min(k, side - k), peer(k)) for k in far for peer in (x_peer, z_peer)]
+    greeted += [(min(k // 2, depth - k // 2), (col, row_peer(k))) for k in far_row]
+    for _, device in sorted(greeted, key=lambda entry: -entry[0]):
+        pl.semaphore_signal(barrier, inc=1, device_id=device, device_id_type=MESH)
 
     loads = [
         pltpu.make_async_copy(source, target, load_sem.at[i])

time: 75.6 us -> 75.6 us (level)
  no operation moved by 1% of the time
where the time goes in v4:
time: 75.6 us; the launch traced here: 75.5 us
  Pallas kernels  74.8 us (99%)
    pallas_call x1, Pallas kernels, on_device(): pl.pallas_call(functools.partial(kernel, side, depth), out_shape=(big, bi...  73.3 us

profile of v4, /device:TPU:2, one launch (start us, length us, event | category | flops | bytes accessed | tf_op | source)
XLA Modules:
  0.0 75.5 jit_solution(11108097970339292885)
XLA Ops:
  0.6 73.3 %dion_step.1 = (f32[512,256]{1,0:T(8,128)S(1)}, f32[512,256]{1,0:T(8,128)S(1)}, f32[512,256]{1,0:T(8,128)S(1)}, f32[256,256]{1,0:T(8,128)S(1)}, f32[2,128]{1,0:T(2,128)S(1)}) custom-call(f32[512,256]{1,0:T(8,128)} %weight_hbm.1, f32[512,256]{1,0:T(8,128)} %momentum_hbm.1, bf16[512,256]{1,0:T(8,128)(2,1)} %gradient_hbm.1, f32[256,256]{1,0:T(8,128)} %factor_hbm.1), custom_call_target="tpu_custom_call" | custom-call | tf_op jit(solution)/shard_map/dion_step/pallas_call | solution.py:407
  74.0 1.5 %dion_finish.1 = (f32[512,256]{1,0:T(8,128)}, f32[512,256]{1,0:T(8,128)}, f32[256,256]{1,0:T(8,128)}) custom-call(f32[512,256]{1,0:T(8,128)S(1)} %get-tuple-element.8.weight, f32[512,256]{1,0:T(8,128)S(1)} %get-tuple-element.9.momentum_now, f32[512,256]{1,0:T(8,128)S(1)} %get-tuple-element.10.left_factor, f32[256,256]{1,0:T(8,128)S(1)} %get-tuple-element.11.right_raw, ...), custom_call_target="tpu_custom_call" | custom-call | tf_op jit(solution)/shard_map/dion_finish/pallas_call | solution.py:418
